TPU v7x, 32 devices: a whole 2x2x4 slice. The times are simulated.
32 devices in a mesh: dp: 8 (over y, x, core), seq: 4 (over z).
Axes of the slice: x: 2, y: 2, z: 4, core: 2. Of those that a mesh axis runs over, the one named last changes fastest.
Arguments:
- tokens: bfloat16 [16, 1024, 512], P('dp', 'seq'), may hold values from -6 to 6
- memory: bfloat16 [16, 1024, 512], P('dp', 'seq'), may hold values from -6 to 6
- tgt_segments: int32 [16, 1024], P('dp'), may hold values from 0 to 2, as said below
- mem_segments: int32 [16, 1024], P('dp'), may hold values from 0 to 2, as said below
- cotangent: bfloat16 [16, 1024, 512], P('dp', 'seq'), may hold values from -6 to 6
- w_qkv: bfloat16 [512, 1536], replicated, may hold values from -0.25 to 0.25
- w_self_out: bfloat16 [512, 512], replicated, may hold values from -1.5 to 1.5
- w_cross_q: bfloat16 [512, 512], replicated, may hold values from -0.25 to 0.25
- w_cross_kv: bfloat16 [512, 1024], replicated, may hold values from -0.25 to 0.25
- w_cross_out: bfloat16 [512, 512], replicated, may hold values from -1.5 to 1.5
- w_up: bfloat16 [512, 2048], replicated, may hold values from -0.25 to 0.25
- w_down: bfloat16 [2048, 512], replicated, may hold values from -0.125 to 0.125
- ln1_gain: float32 [512], replicated, may hold values from 0.25 to 1.75
- ln1_bias: float32 [512], replicated, may hold values from -1.8 to 1.8
- ln2_gain: float32 [512], replicated, may hold values from 0.25 to 1.75
- ln2_bias: float32 [512], replicated, may hold values from -1.8 to 1.8
- ln3_gain: float32 [512], replicated, may hold values from 0.25 to 1.75
- ln3_bias: float32 [512], replicated, may hold values from -1.8 to 1.8
Outputs:
- output: bfloat16 [16, 1024, 512], P('dp', 'seq')
- grad_tokens: float32 [16, 1024, 512], P('dp', 'seq')
- grad_memory: float32 [16, 1024, 512], P('dp', 'seq')
- grad_w_qkv: float32 [512, 1536], replicated
- grad_w_self_out: float32 [512, 512], replicated
- grad_w_cross_q: float32 [512, 512], replicated
- grad_w_cross_kv: float32 [512, 1024], replicated
- grad_w_cross_out: float32 [512, 512], replicated
- grad_w_up: float32 [512, 2048], replicated
- grad_w_down: float32 [2048, 512], replicated
- grad_ln1_gain: float32 [512], replicated
- grad_ln1_bias: float32 [512], replicated
- grad_ln2_gain: float32 [512], replicated
- grad_ln2_bias: float32 [512], replicated
- grad_ln3_gain: float32 [512], replicated
- grad_ln3_bias: float32 [512], replicated
Inputs may be any that keep to these rules, and one draw needn't show every extreme that they name: `tgt_segments`: along a row the ids never fall and all three occur; document 1 begins within the row's first 256 positions and ends within its last 256. `mem_segments`: along a row the ids never fall and all three occur.
All inputs are finite; a program needn't handle non-finite values.
Results may differ from a plain program's by a relative error of at most 0.02.
Values may be sent and summed in bfloat16 or wider, within the bound.
No kernel may reach another device: no remote copies, remote signals or barrier semaphores. Data moves between devices by JAX's collectives and lax.ppermute only.
A program may use at most 128 MiB of HBM per device.

v0:
```python
import math
import jax
import jax.numpy as jnp
from jax import lax
from jax.sharding import PartitionSpec as P

HEAD_DIM = 64


def mat_dot(left, right):
    return jnp.dot(left, right, preferred_element_type=jnp.float32)


def left_dot(left, right):
    return lax.dot_general(
        left, right, (((0,), (0,)), ((), ())), preferred_element_type=jnp.float32
    )


def right_dot(left, right):
    return lax.dot_general(
        left, right, (((1,), (1,)), ((), ())), preferred_element_type=jnp.float32
    )


def layer_norm(values, gain, bias):
    centre = values - jnp.mean(values, axis=-1, keepdims=True)
    recip = lax.rsqrt(jnp.mean(centre * centre, axis=-1, keepdims=True) + 1e-05)
    normed = centre * recip
    return (normed * gain + bias, normed, recip)


def norm_back(grad_out, normed, recip, gain):
    grad_gain = jnp.sum(grad_out * normed, axis=0)
    grad_bias = jnp.sum(grad_out, axis=0)
    scaled = grad_out * gain
    grad_in = recip * (
        scaled
        - jnp.mean(scaled, axis=-1, keepdims=True)
        - normed * jnp.mean(scaled * normed, axis=-1, keepdims=True)
    )
    return (grad_in, grad_gain, grad_bias)


def causal_mask(segment_row):
    place = jnp.arange(segment_row.shape[0])
    return (place[None, :] <= place[:, None]) & (segment_row[:, None] == segment_row[None, :])


def cross_mask(tgt_row, mem_row):
    return tgt_row[:, None] == mem_row[None, :]


def masked_scores(queries, key_heads, allowed, score_scale):
    scores = (
        jnp.einsum("qhd,khd->hqk", queries, key_heads, preferred_element_type=jnp.float32)
        * score_scale
    )
    return jnp.where(allowed[None], scores, -1000000000.0)


def attend_forward(queries, key_heads, value_heads, allowed, score_scale):
    scores = masked_scores(queries, key_heads, allowed, score_scale)
    highest = jnp.max(scores, axis=-1, keepdims=True)
    expo = jnp.exp(scores - highest)
    total = jnp.sum(expo, axis=-1, keepdims=True)
    probs = (expo / total).astype(jnp.bfloat16)
    context = jnp.einsum("hqk,khd->qhd", probs, value_heads, preferred_element_type=jnp.float32)
    return (context.astype(jnp.bfloat16), highest + jnp.log(total))


def attend_backward(queries, key_heads, value_heads, log_total, d_context, allowed, score_scale):
    scores = masked_scores(queries, key_heads, allowed, score_scale)
    probs = jnp.exp(scores - log_total)
    d_values = jnp.einsum(
        "hqk,qhd->khd", probs.astype(jnp.bfloat16), d_context, preferred_element_type=jnp.float32
    ).astype(jnp.bfloat16)
    d_probs = jnp.einsum("qhd,khd->hqk", d_context, value_heads, preferred_element_type=jnp.float32)
    centre = jnp.sum(probs * d_probs, axis=-1, keepdims=True)
    d_scores = (probs * (d_probs - centre)).astype(jnp.bfloat16)
    d_queries = (
        jnp.einsum("hqk,khd->qhd", d_scores, key_heads, preferred_element_type=jnp.float32)
        * score_scale
    ).astype(jnp.bfloat16)
    d_keys = (
        jnp.einsum("hqk,qhd->khd", d_scores, queries, preferred_element_type=jnp.float32)
        * score_scale
    ).astype(jnp.bfloat16)
    return (d_queries, d_keys, d_values)


def body(
    tokens,
    memory,
    tgt_segments,
    mem_segments,
    cotangent,
    w_qkv,
    w_self_out,
    w_cross_q,
    w_cross_kv,
    w_cross_out,
    w_up,
    w_down,
    ln1_gain,
    ln1_bias,
    ln2_gain,
    ln2_bias,
    ln3_gain,
    ln3_bias,
):
    row_count, tok_local, model_width = tokens.shape
    mem_local = memory.shape[1]
    seq_parts = lax.axis_size("seq")
    head_share = model_width // seq_parts
    heads_here = head_share // HEAD_DIM
    seq_len = tgt_segments.shape[1]
    mem_len = mem_segments.shape[1]
    score_scale = 1.0 / math.sqrt(HEAD_DIM)
    token_total = row_count * tok_local
    flat_tokens = tokens.reshape(token_total, model_width)
    flat_memory = memory.reshape(row_count * mem_local, model_width)
    mixed_proj = (
        mat_dot(flat_tokens, w_qkv)
        .astype(jnp.bfloat16)
        .reshape(row_count, tok_local, 3, seq_parts, head_share)
    )
    self_heads = lax.all_to_all(mixed_proj, "seq", split_axis=3, concat_axis=1, tiled=True).reshape(
        row_count, seq_len, 3, heads_here, HEAD_DIM
    )
    memory_proj = (
        mat_dot(flat_memory, w_cross_kv)
        .astype(jnp.bfloat16)
        .reshape(row_count, mem_local, 2, seq_parts, head_share)
    )
    memory_heads = lax.all_to_all(
        memory_proj, "seq", split_axis=3, concat_axis=1, tiled=True
    ).reshape(row_count, mem_len, 2, heads_here, HEAD_DIM)
    self_q = self_heads[:, :, 0]
    self_k = self_heads[:, :, 1]
    self_v = self_heads[:, :, 2]
    memory_k = memory_heads[:, :, 0]
    memory_v = memory_heads[:, :, 1]

    def self_forward(row_item):
        queries, key_heads, value_heads, segment_row = row_item
        return attend_forward(
            queries, key_heads, value_heads, causal_mask(segment_row), score_scale
        )

    self_context, self_lse = lax.map(self_forward, (self_q, self_k, self_v, tgt_segments))
    self_back = lax.all_to_all(
        self_context.reshape(row_count, seq_len, 1, head_share),
        "seq",
        split_axis=1,
        concat_axis=2,
        tiled=True,
    )
    context_one = self_back.reshape(token_total, model_width)
    attn_one = mat_dot(context_one, w_self_out)
    norm_one, normed_one, recip_one = layer_norm(
        flat_tokens.astype(jnp.float32) + attn_one, ln1_gain, ln1_bias
    )
    norm_one_low = norm_one.astype(jnp.bfloat16)
    cross_proj = (
        mat_dot(norm_one_low, w_cross_q)
        .astype(jnp.bfloat16)
        .reshape(row_count, tok_local, 1, seq_parts, head_share)
    )
    cross_q = lax.all_to_all(cross_proj, "seq", split_axis=3, concat_axis=1, tiled=True).reshape(
        row_count, seq_len, heads_here, HEAD_DIM
    )

    def cross_forward(row_item):
        queries, key_heads, value_heads, tgt_row, mem_row = row_item
        return attend_forward(
            queries, key_heads, value_heads, cross_mask(tgt_row, mem_row), score_scale
        )

    cross_context, cross_lse = lax.map(
        cross_forward, (cross_q, memory_k, memory_v, tgt_segments, mem_segments)
    )
    cross_back = lax.all_to_all(
        cross_context.reshape(row_count, seq_len, 1, head_share),
        "seq",
        split_axis=1,
        concat_axis=2,
        tiled=True,
    )
    context_two = cross_back.reshape(token_total, model_width)
    attn_two = mat_dot(context_two, w_cross_out)
    norm_two, normed_two, recip_two = layer_norm(norm_one + attn_two, ln2_gain, ln2_bias)
    norm_two_low = norm_two.astype(jnp.bfloat16)
    pre_act = mat_dot(norm_two_low, w_up)
    sigma = jax.nn.sigmoid(pre_act)
    hidden_low = (pre_act * sigma).astype(jnp.bfloat16)
    fed = mat_dot(hidden_low, w_down)
    result, normed_three, recip_three = layer_norm(norm_two + fed, ln3_gain, ln3_bias)
    output = result.astype(jnp.bfloat16).reshape(row_count, tok_local, model_width)
    grad_out = cotangent.reshape(token_total, model_width).astype(jnp.float32)
    d_resid_three, d_gain_three, d_bias_three = norm_back(
        grad_out, normed_three, recip_three, ln3_gain
    )
    d_fed_low = d_resid_three.astype(jnp.bfloat16)
    grad_down = left_dot(hidden_low, d_fed_low)
    d_hidden = right_dot(d_fed_low, w_down)
    d_pre_low = (d_hidden * sigma * (1.0 + pre_act * (1.0 - sigma))).astype(jnp.bfloat16)
    grad_up = left_dot(norm_two_low, d_pre_low)
    d_norm_two = d_resid_three + right_dot(d_pre_low, w_up)
    d_resid_two, d_gain_two, d_bias_two = norm_back(d_norm_two, normed_two, recip_two, ln2_gain)
    d_attn_two = d_resid_two.astype(jnp.bfloat16)
    grad_cross_out = left_dot(context_two, d_attn_two)
    d_context_two = (
        right_dot(d_attn_two, w_cross_out)
        .astype(jnp.bfloat16)
        .reshape(row_count, tok_local, seq_parts, head_share)
    )
    d_cross_heads = lax.all_to_all(
        d_context_two, "seq", split_axis=2, concat_axis=1, tiled=True
    ).reshape(row_count, seq_len, heads_here, HEAD_DIM)

    def cross_backward(row_item):
        queries, key_heads, value_heads, log_total, d_context, tgt_row, mem_row = row_item
        return attend_backward(
            queries,
            key_heads,
            value_heads,
            log_total,
            d_context,
            cross_mask(tgt_row, mem_row),
            score_scale,
        )

    d_cross_q, d_mem_keys, d_mem_values = lax.map(
        cross_backward,
        (cross_q, memory_k, memory_v, cross_lse, d_cross_heads, tgt_segments, mem_segments),
    )
    d_memory_kv = jnp.stack((d_mem_keys, d_mem_values), axis=2).reshape(
        row_count, mem_len, 2, 1, head_share
    )
    back_query, back_memory = (
        lax.all_to_all(
            d_cross_q.reshape(row_count, seq_len, 1, 1, head_share),
            "seq",
            split_axis=1,
            concat_axis=3,
            tiled=True,
        ),
        lax.all_to_all(d_memory_kv, "seq", split_axis=1, concat_axis=3, tiled=True),
    )
    d_query_flat = back_query.reshape(token_total, model_width)
    d_memory_flat = back_memory.reshape(row_count * mem_local, 2 * model_width)
    grad_cross_q = left_dot(norm_one_low, d_query_flat)
    grad_cross_kv = left_dot(flat_memory, d_memory_flat)
    grad_memory = right_dot(d_memory_flat, w_cross_kv).reshape(row_count, mem_local, model_width)
    d_norm_one = d_resid_two + right_dot(d_query_flat, w_cross_q)
    d_resid_one, d_gain_one, d_bias_one = norm_back(d_norm_one, normed_one, recip_one, ln1_gain)
    d_attn_one = d_resid_one.astype(jnp.bfloat16)
    grad_self_out = left_dot(context_one, d_attn_one)
    d_context_one = (
        right_dot(d_attn_one, w_self_out)
        .astype(jnp.bfloat16)
        .reshape(row_count, tok_local, seq_parts, head_share)
    )
    d_self_heads = lax.all_to_all(
        d_context_one, "seq", split_axis=2, concat_axis=1, tiled=True
    ).reshape(row_count, seq_len, heads_here, HEAD_DIM)

    def self_backward(row_item):
        queries, key_heads, value_heads, log_total, d_context, segment_row = row_item
        return attend_backward(
            queries,
            key_heads,
            value_heads,
            log_total,
            d_context,
            causal_mask(segment_row),
            score_scale,
        )

    d_self_q, d_self_k, d_self_v = lax.map(
        self_backward, (self_q, self_k, self_v, self_lse, d_self_heads, tgt_segments)
    )
    d_mixed = jnp.stack((d_self_q, d_self_k, d_self_v), axis=2).reshape(
        row_count, seq_len, 3, 1, head_share
    )
    back_mixed = lax.all_to_all(d_mixed, "seq", split_axis=1, concat_axis=3, tiled=True).reshape(
        token_total, 3 * model_width
    )
    grad_qkv = left_dot(flat_tokens, back_mixed)
    grad_tokens = (d_resid_one + right_dot(back_mixed, w_qkv)).reshape(
        row_count, tok_local, model_width
    )
    summed = lax.psum(
        (
            grad_qkv,
            grad_self_out,
            grad_cross_q,
            grad_cross_kv,
            grad_cross_out,
            grad_up,
            grad_down,
            d_gain_one,
            d_bias_one,
            d_gain_two,
            d_bias_two,
            d_gain_three,
            d_bias_three,
        ),
        ("dp", "seq"),
    )
    return (
        output,
        grad_tokens,
        grad_memory,
        summed[0],
        summed[1],
        summed[2],
        summed[3],
        summed[4],
        summed[5],
        summed[6],
        summed[7],
        summed[8],
        summed[9],
        summed[10],
        summed[11],
        summed[12],
    )


def solution(mesh):
    return jax.shard_map(
        body,
        mesh=mesh,
        in_specs=(
            P("dp", "seq", None),
            P("dp", "seq", None),
            P("dp", None),
            P("dp", None),
            P("dp", "seq", None),
            P(),
            P(),
            P(),
            P(),
            P(),
            P(),
            P(),
            P(),
            P(),
            P(),
            P(),
            P(),
            P(),
        ),
        out_specs=(
            P("dp", "seq", None),
            P("dp", "seq", None),
            P("dp", "seq", None),
            P(),
            P(),
            P(),
            P(),
            P(),
            P(),
            P(),
            P(),
            P(),
            P(),
            P(),
            P(),
            P(),
        ),
        check_vma=False,
    )
```

profile of v0, /device:TPU:0, one launch (start us, length us, event | category | flops | bytes accessed | tf_op | source)
XLA Modules:
  0.0 717.0 jit_solution(7663693203559814328)
XLA Ops:
  7.2 3.8 convolution_convert_fusion
  11.0 3.9 reshape.401
  15.0 2.9 copy.196
  17.9 6.3 all-to-all-start
  24.2 37.1 %all-to-all-done = bf16[2,256,3,4,128]{4,1,2,0,3:T(8,128)(2,1)} async-done(((bf16[2,256,3,4,128]{4,1,2,0,3:T(8,128)(2,1)}), bf16[2,256,3,4,128]{4,1,2,0,3:T(8,128)(2,1)}, u32[]{:S(2)}, u32[]{:S(2)}) %all-to-all-start) | async-done | bytes 1572896 | tf_op jit(solution)/shard_map/all_to_all | solution.py:128
  61.3 3.8 copy.197
  65.0 3.8 reshape.402
  72.0 16.4 %while.52 = (s32[]{:T(128)}, bf16[2,1024,2,64]{1,3,2,0:T(8,128)(2,1)}, f32[2,2,1024,1]{2,1,3,0:T(2,128)S(1)}, bf16[2,1024,2,64]{1,3,2,0:T(8,128)(2,1)}, s32[2,10...) while((s32[]{:T(128)}, ...), condition=%wide.region_3.4_spmd, body=%wide.region_0.3_spmd.sunk | while | flops 565311488 | bytes 36780216 | solution.py:151
  76.6 2.8 fusion.227
  84.8 2.8 fusion.227
  90.7 4.1 all-to-all-start.1
  94.8 3.1 convolution_convert_fusion.1
  97.9 2.6 reshape.406
  100.5 3.0 copy.201
  103.5 5.4 all-to-all-done.1
  108.9 4.3 all-to-all-start.2
  122.7 15.7 %all-to-all-done.2 = bf16[2,256,2,4,128]{4,2,1,0,3:T(2,128)(2,1)} async-done(((bf16[2,256,2,4,128]{4,2,1,0,3:T(2,128)(2,1)}), bf16[2,256,2,4,128]{4,2,1,0,3:T(2,128)(2,1)}, u32[]{:S(2)}, u32[]{:S(2)}) %all-to-all-start.2) | async-done | bytes 1048608 | tf_op jit(solution)/shard_map/all_to_all | solution.py:136
  138.4 4.4 all-to-all-start.3
  142.9 3.8 copy.202
  146.7 2.6 reshape.407
  151.5 5.4 all-to-all-done.3
  162.1 18.5 %while.53 = (s32[]{:T(128)}, bf16[2,1024,2,64]{1,3,2,0:T(8,128)(2,1)}, f32[2,2,1024,1]{2,1,3,0:T(2,128)S(1)}, bf16[2,1024,2,64]{1,3,2,0:T(8,128)(2,1)}, s32[2,10...) while((s32[]{:T(128)}, ...), condition=%wide.region_9.10_spmd, body=%wide.region_6.9_spmd.sunk | while | flops 563214336 | bytes 36792512 | solution.py:180
  162.8 2.9 fusion.229
  167.7 2.8 fusion.231
  172.0 2.9 fusion.229
  177.0 2.8 fusion.231
  182.6 4.8 all-to-all-start.4
  189.4 12.1 %all-to-all-done.4 = bf16[2,1024,1,128]{3,0,2,1:T(2,128)(2,1)} async-done(((bf16[2,1024,1,128]{3,0,2,1:T(2,128)(2,1)}), bf16[2,1024,1,128]{3,0,2,1:T(2,128)(2,1)}, u32[]{:S(2)}, u32[]{:S(2)}) %all-to-all-start.4) | async-done | bytes 524320 | tf_op jit(solution)/shard_map/all_to_all | solution.py:183
  221.2 4.3 all-to-all-start.5
  225.5 14.1 %all-to-all-done.5 = bf16[2,256,4,128]{3,1,0,2:T(8,128)(2,1)} async-done(((bf16[2,256,4,128]{3,1,0,2:T(8,128)(2,1)}), bf16[2,256,4,128]{3,1,0,2:T(8,128)(2,1)}, u32[]{:S(2)}, u32[]{:S(2)}) %all-to-all-start.5) | async-done | bytes 524320 | tf_op jit(solution)/shard_map/all_to_all | solution.py:218
  246.6 27.1 %while.54 = (s32[]{:T(128)}, bf16[2,1024,2,64]{1,3,2,0:T(8,128)(2,1)}, bf16[2,1024,2,64]{1,3,2,0:T(8,128)(2,1)}, bf16[2,1024,2,64]{1,3,2,0:T(8,128)(2,1)}, bf16[...) while((s32[]{:T(128)}, ...), condition=%wide.region_20.21_spmd, body=%wide.region_18.20_spmd.sunk | while | flops 1375336448 | bytes 86594928 | solution.py:234
  248.6 3.0 multiply_reduce_fusion.13
  251.6 2.7 multiply_convert_fusion.8
  256.8 2.5 fusion.243
  262.2 3.0 multiply_reduce_fusion.13
  265.2 2.7 multiply_convert_fusion.8
  270.4 2.5 fusion.243
  275.1 16.4 %all_to_all.150 = bf16[2,1024,1,1,128]{4,0,3,2,1:T(2,128)(2,1)S(1)} all-to-all(bf16[2,1024,1,1,128]{4,0,3,2,1:T(2,128)(2,1)S(1)} %copy.210), channel_id=1, replica_groups=mesh['dp'=8,'seq'=4] {'seq'}, dimensions={1} | all-to-all | bytes 1048576 | tf_op jit(solution)/shard_map/all_to_all | solution.py:242
  296.0 4.1 all-to-all-start.7
  303.5 10.2 %all-to-all-done.7 = bf16[2,256,4,128]{3,1,0,2:T(8,128)(2,1)} async-done(((bf16[2,256,4,128]{3,1,0,2:T(8,128)(2,1)}), bf16[2,256,4,128]{3,1,0,2:T(8,128)(2,1)}, u32[]{:S(2)}, u32[]{:S(2)}) %all-to-all-start.7) | async-done | bytes 524320 | tf_op jit(solution)/shard_map/all_to_all | solution.py:265
  313.7 4.5 all-to-all-start.9
  323.4 27.0 %while.55 = (s32[]{:T(128)}, bf16[2,1024,2,64]{1,3,2,0:T(8,128)(2,1)}, bf16[2,1024,2,64]{1,3,2,0:T(8,128)(2,1)}, bf16[2,1024,2,64]{1,3,2,0:T(8,128)(2,1)}, bf16[...) while((s32[]{:T(128)}, ...), condition=%wide.region_25.26_spmd, body=%wide.region_23.25_spmd.sunk | while | flops 1377433600 | bytes 86582632 | solution.py:281
  325.4 3.0 multiply_reduce_fusion.14
  328.4 2.7 multiply_convert_fusion.9
  333.5 2.5 fusion.256
  338.9 3.0 multiply_reduce_fusion.14
  341.9 2.7 multiply_convert_fusion.9
  347.0 2.5 fusion.256
  350.4 2.8 pad_maximum_fusion
  353.2 5.0 copy.215
  358.2 5.1 all-to-all-start.8
  363.7 2.5 fusion.134
  366.2 5.2 fusion.153
  371.4 3.5 fusion.150
  383.1 16.2 %all-to-all-done.8 = bf16[2,1024,3,1,128]{4,0,3,2,1:T(2,128)(2,1)} async-done(((bf16[2,1024,3,1,128]{4,0,3,2,1:T(2,128)(2,1)}), bf16[2,1024,3,1,128]{4,0,3,2,1:T(2,128)(2,1)}, u32[]{:S(2)}, u32[]{:S(2)}) %all-to-all-start.8) | async-done | bytes 1572896 | tf_op jit(solution)/shard_map/all_to_all | solution.py:287
  400.9 2.4 copy.217
  403.3 2.8 reshape.419
  406.1 2.7 convolution_bitcast_fusion
  409.5 40.1 %all-reduce = (f32[512]{0:T(512)}, f32[512]{0:T(512)}, f32[512]{0:T(512)}, f32[512]{0:T(512)}, f32[512]{0:T(512)}, /*index=5*/f32[512]{0:T(512)}) all-reduce(f32[512]{0:T(512)S(1)} %get-tuple-element.334, f32[512]{0:T(512)S(1)} %get-tuple-element.341, f32[512]{0:T(512)S(1)} %copy-done.74, ...), channel_id=1, replica_groups=mesh['dp'=8,'seq'=4] {'dp','seq'}, use_global_device_ids=true, to_apply=%region_34.35 | all-reduce | flops 3072 | bytes 24576 | tf_op jit(solution)/shard_map/psum | solution.py:294
  451.2 3.3 fusion.120
  454.5 3.8 convolution_add_fusion.3
  458.3 234.8 %all-reduce.4.cloned.1.call-done = (f32[512,1536]{0,1:T(8,128)}, f32[512,512]{1,0:T(8,128)}, f32[512,512]{1,0:T(8,128)}, f32[512,1024]{0,1:T(8,128)}, f32[512,51...) async-done(((f32[512,1536]{0,1:T(8,128)}, f32[512,512]{1,0:T(8,128)}, f32[512,512]{1,0:T(8,128)}, f32[512,1024]{0,1:T(8,128)}, f32[512,512]{1,0:T(8,128)}, ...) | async-done | bytes 16777232 | tf_op jit(solution)/shard_map/psum | solution.py:294
  693.1 3.7 copy.222
  698.6 2.4 copy.327
  (325 shorter events, 128.5 us)
Async XLA Ops:
  7.2 198.6 %copy-start = (bf16[512,2048]{1,0:T(8,128)(2,1)S(1)}, bf16[512,2048]{1,0:T(8,128)(2,1)}, u32[]{:S(2)}) copy-start(bf16[512,2048]{1,0:T(8,128)(2,1)} %param.36) | copy-start | bytes 6291460
  17.9 43.4 %all-to-all-start = ((bf16[2,256,3,4,128]{4,1,2,0,3:T(8,128)(2,1)}), bf16[2,256,3,4,128]{4,1,2,0,3:T(8,128)(2,1)}, u32[]{:S(2)}, u32[]{:S(2)}) async-start(bf16[2,256,3,4,128]{4,1,2,0,3:T(8,128)(2,1)} %copy.196), calls=%async_computation | async-start | bytes 3145728 | tf_op jit(solution)/shard_map/all_to_all | solution.py:128
  65.0 7.0 copy-start.55
  88.4 15.1 %copy-start.5 = (bf16[2,1024,2,64]{1,3,2,0:T(8,128)(2,1)}, bf16[2,1024,2,64]{1,3,2,0:T(8,128)(2,1)S(1)}, u32[]{:S(2)}) copy-start(bf16[2,1024,2,64]{1,3,2,0:T(8,128)(2,1)S(1)} %get-tuple-element.855) | copy-start | bytes 1572868
  88.4 15.1 %copy-start.7 = (bf16[2,1024,2,64]{1,3,2,0:T(8,128)(2,1)}, bf16[2,1024,2,64]{1,3,2,0:T(8,128)(2,1)S(1)}, u32[]{:S(2)}) copy-start(bf16[2,1024,2,64]{1,3,2,0:T(8,128)(2,1)S(1)} %get-tuple-element.856) | copy-start | bytes 1572868
  88.4 15.1 %copy-start.59 = (f32[2,2,1024,1]{2,1,3,0:T(2,128)}, f32[2,2,1024,1]{2,1,3,0:T(2,128)S(1)}, u32[]{:S(2)}) copy-start(f32[2,2,1024,1]{2,1,3,0:T(2,128)S(1)} %get-tuple-element.796) | copy-start | bytes 49156
  90.7 18.2 %all-to-all-start.1 = ((bf16[2,1024,1,128]{3,0,2,1:T(2,128)(2,1)}), bf16[2,1024,1,128]{3,0,2,1:T(2,128)(2,1)}, u32[]{:S(2)}, u32[]{:S(2)}) async-start(bf16[2,1024,1,128]{3,0,2,1:T(2,128)(2,1)} %copy.198), calls=%async_computation.1 | async-start | bytes 1048576 | tf_op jit(solution)/shard_map/all_to_all | solution.py:152
  103.5 14.1 %copy-start.70 = (f32[512]{0:T(512)S(1)}, f32[512]{0:T(512)}, u32[]{:S(2)}) copy-start(f32[512]{0:T(512)} %param.38) | copy-start | bytes 6148
  103.5 14.1 %copy-start.76 = (f32[512]{0:T(512)S(1)}, f32[512]{0:T(512)}, u32[]{:S(2)}) copy-start(f32[512]{0:T(512)} %param.39) | copy-start | bytes 6148
  108.9 29.5 %all-to-all-start.2 = ((bf16[2,256,2,4,128]{4,2,1,0,3:T(2,128)(2,1)}), bf16[2,256,2,4,128]{4,2,1,0,3:T(2,128)(2,1)}, u32[]{:S(2)}, u32[]{:S(2)}) async-start(bf16[2,256,2,4,128]{4,2,1,0,3:T(2,128)(2,1)} %copy.201), calls=%async_computation.2 | async-start | bytes 2097152 | tf_op jit(solution)/shard_map/all_to_all | solution.py:136
  113.2 4.4 copy-start.56
  138.4 18.5 %all-to-all-start.3 = ((bf16[2,256,1,4,128]{4,1,0,2,3:T(8,128)(2,1)}), bf16[2,256,1,4,128]{4,1,0,2,3:T(8,128)(2,1)}, u32[]{:S(2)}, u32[]{:S(2)}) async-start(bf16[2,256,1,4,128]{4,1,0,2,3:T(8,128)(2,1)} %copy.203), calls=%async_computation.3 | async-start | bytes 1048576 | tf_op jit(solution)/shard_map/all_to_all | solution.py:170
  142.9 19.2 %copy-start.58 = (s32[2,1024]{1,0:T(2,128)S(1)}, s32[2,1024]{1,0:T(2,128)}, u32[]{:S(2)}) copy-start(s32[2,1024]{1,0:T(2,128)} %param.29) | copy-start | bytes 24580
  162.1 25.4 %copy-start.69 = (f32[512]{0:T(512)S(1)}, f32[512]{0:T(512)}, u32[]{:S(2)}) copy-start(f32[512]{0:T(512)} %param.42) | copy-start | bytes 6148
  182.6 23.2 %copy-start.65 = (f32[512]{0:T(512)S(1)}, f32[512]{0:T(512)}, u32[]{:S(2)}) copy-start(f32[512]{0:T(512)} %param.40) | copy-start | bytes 6148
  182.6 23.2 %copy-start.67 = (f32[512]{0:T(512)S(1)}, f32[512]{0:T(512)}, u32[]{:S(2)}) copy-start(f32[512]{0:T(512)} %param.41) | copy-start | bytes 6148
  182.6 18.9 %all-to-all-start.4 = ((bf16[2,1024,1,128]{3,0,2,1:T(2,128)(2,1)}), bf16[2,1024,1,128]{3,0,2,1:T(2,128)(2,1)}, u32[]{:S(2)}, u32[]{:S(2)}) async-start(bf16[2,1024,1,128]{3,0,2,1:T(2,128)(2,1)} %copy.205), calls=%async_computation.4 | async-start | bytes 1048576 | tf_op jit(solution)/shard_map/all_to_all | solution.py:183
  205.5 10.1 %copy-start.2 = (f32[512,512]{1,0:T(8,128)}, f32[512,512]{1,0:T(8,128)S(1)}, u32[]{:S(2)}) copy-start(f32[512,512]{1,0:T(8,128)S(1)} %get-tuple-element.451) | copy-start | bytes 3145732
  205.5 10.1 %copy-start.61 = (f32[512]{0:T(512)}, f32[512]{0:T(512)S(1)}, u32[]{:S(2)}) copy-start(f32[512]{0:T(512)S(1)} %broadcast_multiply_fusion.6) | copy-start | bytes 6148
  205.8 9.8 %copy-start.63 = (f32[512]{0:T(512)}, f32[512]{0:T(512)S(1)}, u32[]{:S(2)}) copy-start(f32[512]{0:T(512)S(1)} %add_rsqrt_fusion.1) | copy-start | bytes 6148
  207.5 4.0 copy-start.25
  207.5 2.8 copy-start.73
  216.0 29.8 %copy-start.10 = (f32[512,512]{1,0:T(8,128)}, f32[512,512]{1,0:T(8,128)S(1)}, u32[]{:S(2)}) copy-start(f32[512,512]{1,0:T(8,128)S(1)} %subtract_multiply_fusion.1) | copy-start | bytes 3145732
  216.0 30.6 %copy-start.4 = (bf16[2,1024,2,64]{1,3,2,0:T(8,128)(2,1)S(1)}, bf16[2,1024,2,64]{1,3,2,0:T(8,128)(2,1)}, u32[]{:S(2)}) copy-start(bf16[2,1024,2,64]{1,3,2,0:T(8,128)(2,1)} %get-tuple-element.854) | copy-start | bytes 1572868
  216.0 30.6 %copy-start.9 = (bf16[2,1024,2,64]{1,3,2,0:T(8,128)(2,1)S(1)}, bf16[2,1024,2,64]{1,3,2,0:T(8,128)(2,1)}, u32[]{:S(2)}) copy-start(bf16[2,1024,2,64]{1,3,2,0:T(8,128)(2,1)} %get-tuple-element.857) | copy-start | bytes 1572868
  221.2 18.4 %all-to-all-start.5 = ((bf16[2,256,4,128]{3,1,0,2:T(8,128)(2,1)}), bf16[2,256,4,128]{3,1,0,2:T(8,128)(2,1)}, u32[]{:S(2)}, u32[]{:S(2)}) async-start(bf16[2,256,4,128]{3,1,0,2:T(8,128)(2,1)} %copy.208), calls=%async_computation.5 | async-start | bytes 1048576 | tf_op jit(solution)/shard_map/all_to_all | solution.py:218
  251.6 2.7 copy-start.32
  255.2 4.1 copy-start.33
  265.2 2.7 copy-start.32
  268.8 4.1 copy-start.33
  273.7 18.3 %copy-start.11 = (f32[512,512]{1,0:T(8,128)S(1)}, f32[512,512]{1,0:T(8,128)}, u32[]{:S(2)}) copy-start(f32[512,512]{1,0:T(8,128)} %copy-done.10) | copy-start | bytes 3145732
  291.6 2.9 copy-start.50
  294.5 5.7 copy-start.13
  296.0 17.8 %all-to-all-start.7 = ((bf16[2,256,4,128]{3,1,0,2:T(8,128)(2,1)}), bf16[2,256,4,128]{3,1,0,2:T(8,128)(2,1)}, u32[]{:S(2)}, u32[]{:S(2)}) async-start(bf16[2,256,4,128]{3,1,0,2:T(8,128)(2,1)} %copy.213), calls=%async_computation.7 | async-start | bytes 1048576 | tf_op jit(solution)/shard_map/all_to_all | solution.py:265
  301.4 21.9 %copy-start.6 = (bf16[2,1024,2,64]{1,3,2,0:T(8,128)(2,1)S(1)}, bf16[2,1024,2,64]{1,3,2,0:T(8,128)(2,1)}, u32[]{:S(2)}) copy-start(bf16[2,1024,2,64]{1,3,2,0:T(8,128)(2,1)} %copy-done.5) | copy-start | bytes 1572868
  301.4 21.9 %copy-start.8 = (bf16[2,1024,2,64]{1,3,2,0:T(8,128)(2,1)S(1)}, bf16[2,1024,2,64]{1,3,2,0:T(8,128)(2,1)}, u32[]{:S(2)}) copy-start(bf16[2,1024,2,64]{1,3,2,0:T(8,128)(2,1)} %copy-done.7) | copy-start | bytes 1572868
  301.5 21.9 %copy-start.60 = (f32[2,2,1024,1]{2,1,3,0:T(2,128)S(1)}, f32[2,2,1024,1]{2,1,3,0:T(2,128)}, u32[]{:S(2)}) copy-start(f32[2,2,1024,1]{2,1,3,0:T(2,128)} %copy-done.59) | copy-start | bytes 49156
  313.7 44.5 %all-to-all-start.9 = ((bf16[2,1024,2,1,128]{4,0,3,2,1:T(2,128)(2,1)}), bf16[2,1024,2,1,128]{4,0,3,2,1:T(2,128)(2,1)}, u32[]{:S(2)}, u32[]{:S(2)}) async-start(bf16[2,1024,2,1,128]{4,0,3,2,1:T(2,128)(2,1)} %copy.218), calls=%async_computation.9 | async-start | bytes 2097152 | tf_op jit(solution)/shard_map/all_to_all | solution.py:249
  328.4 2.7 copy-start.38
  332.0 4.1 copy-start.39
  333.5 2.6 copy-start.41
  341.9 2.7 copy-start.38
  345.5 4.1 copy-start.39
  350.4 13.3 %copy-start.12 = (f32[512,512]{1,0:T(8,128)S(1)}, f32[512,512]{1,0:T(8,128)}, u32[]{:S(2)}) copy-start(f32[512,512]{1,0:T(8,128)} %copy-done.10) | copy-start | bytes 3145732
  353.2 13.0 %copy-start.3 = (f32[512,512]{1,0:T(8,128)S(1)}, f32[512,512]{1,0:T(8,128)}, u32[]{:S(2)}) copy-start(f32[512,512]{1,0:T(8,128)} %copy-done.2) | copy-start | bytes 3145732
  353.2 13.0 %copy-start.62 = (f32[512]{0:T(512)S(1)}, f32[512]{0:T(512)}, u32[]{:S(2)}) copy-start(f32[512]{0:T(512)} %copy-done.61) | copy-start | bytes 6148
  353.2 13.0 %copy-start.64 = (f32[512]{0:T(512)S(1)}, f32[512]{0:T(512)}, u32[]{:S(2)}) copy-start(f32[512]{0:T(512)} %copy-done.63) | copy-start | bytes 6148
  353.2 13.0 %copy-start.66 = (f32[512]{0:T(512)S(1)}, f32[512]{0:T(512)}, u32[]{:S(2)}) copy-start(f32[512]{0:T(512)} %param.40) | copy-start | bytes 6148
  353.2 13.0 %copy-start.68 = (f32[512]{0:T(512)S(1)}, f32[512]{0:T(512)}, u32[]{:S(2)}) copy-start(f32[512]{0:T(512)} %param.41) | copy-start | bytes 6148
  358.2 41.1 %all-to-all-start.8 = ((bf16[2,1024,3,1,128]{4,0,3,2,1:T(2,128)(2,1)}), bf16[2,1024,3,1,128]{4,0,3,2,1:T(2,128)(2,1)}, u32[]{:S(2)}, u32[]{:S(2)}) async-start(bf16[2,1024,3,1,128]{4,0,3,2,1:T(2,128)(2,1)} %copy.215), calls=%async_computation.8 | async-start | bytes 3145728 | tf_op jit(solution)/shard_map/all_to_all | solution.py:287
  363.3 329.8 %all-reduce.4.cloned.1.call-start = ((), (), s32[]{:S(2)}) async-start(), calls=%async_computation.10 | async-start | bytes 33554432 | tf_op jit(solution)/shard_map/psum | solution.py:294
  366.2 5.2 copy-start.26
  366.2 5.2 copy-start.53
  371.4 3.5 copy-start.14
  371.4 3.5 copy-start.22
  371.4 4.9 copy-start.30
  371.4 4.9 copy-start.77
  376.3 4.6 copy-start.57
  383.1 23.1 %copy-start.51 = (bf16[2,256,512]{2,1,0:T(8,128)(2,1)S(1)}, bf16[2,256,512]{2,1,0:T(8,128)(2,1)}, u32[]{:S(2)}) copy-start(bf16[2,256,512]{2,1,0:T(8,128)(2,1)} %param.26) | copy-start | bytes 1572868
  693.1 3.7 copy-start.31
  696.7 6.5 copy-start.54
  698.6 5.7 copy-start.28
  704.2 3.7 copy-start.27
  704.2 5.7 copy-start.1
  (47 other events, 77.2 us)
Sparse Core Ops, SparseCore 0:
  409.0 284.0 all-reduce.3
where the time goes:
time: 728 us; the launch traced here: 717 us
  waiting for transfers between devices  351 us (48%)
  local copies, waits for them, and re-layouts  112 us (15%)
  matrix products  105 us (14%)
  blocking collectives  56.5 us (8%)
  starting transfers between devices  42.4 us (6%)
  other arithmetic  33.6 us (5%)
  between operations  14.9 us (2%)
    psum x1, waiting for transfers between devices, body(): lax.psum((grad_qkv, grad_self_out, grad_cross_q, grad_cross_kv, grad_cros...  235 us
    psum x1, blocking collectives, body(): lax.psum((grad_qkv, grad_self_out, grad_cross_q, grad_cross_kv, grad_cros...  40.1 us
    all_to_all x1, waiting for transfers between devices, body(): lax.all_to_all(mixed_proj, 'seq', split_axis=3, concat_axis=1, tiled=True)  37.1 us
    unnamed x122, local copies, waits for them, and re-layouts  19.7 us
    dot_general x7, matrix products, left_dot(): lax.dot_general(left, right, (((0,), (0,)), ((), ())), preferred_element_...  19 us
    all_to_all x1, blocking collectives, body(): lax.all_to_all(d_cross_q.reshape(row_count, seq_len, 1, 1, head_share), '...  16.4 us
    all_to_all x1, waiting for transfers between devices, body(): lax.all_to_all(d_mixed, 'seq', split_axis=1, concat_axis=3, tiled=True)  16.2 us
    all_to_all x1, waiting for transfers between devices, body(): lax.all_to_all(memory_proj, 'seq', split_axis=3, concat_axis=1, tiled=True)  15.7 us
  transfers between devices with their start and end apart: 10, of which 9 were waited for; matrix products, arithmetic and copies ran while one was open for 14% of the time, Pallas kernels for 0%

commit v1 on v0

--- a/solution.py
+++ b/solution.py
@@ -239,12 +239,20 @@
         row_count, mem_len, 2, 1, head_share
     )
     back_query, back_memory = (
-        lax.all_to_all(
-            d_cross_q.reshape(row_count, seq_len, 1, 1, head_share),
-            "seq",
-            split_axis=1,
-            concat_axis=3,
-            tiled=True,
+        jnp.concatenate(
+            lax.all_to_all(
+                jnp.stack(
+                    jnp.split(
+                        d_cross_q.reshape(row_count, seq_len, 1, 1, head_share),
+                        lax.axis_size("seq"),
+                        axis=1,
+                    )
+                ),
+                "seq",
+                0,
+                0,
+            ),
+            axis=3,
         ),
         lax.all_to_all(d_memory_kv, "seq", split_axis=1, concat_axis=3, tiled=True),
     )

time: 728 us -> 730 us (level)
    unnamed x122 -> x116, local copies, waits for them, and re-layouts: 19.7 us -> 19.7 us
  transfers between devices with their start and end apart: 10 -> 10, of which waited for: 9 -> 9; matrix products, arithmetic and copies ran while one was open for 14% -> 13% of each run, Pallas kernels for 0% -> 0%
where the time goes in v1:
time: 730 us; the launch traced here: 719 us
  waiting for transfers between devices  352 us (48%)
  local copies, waits for them, and re-layouts  110 us (15%)
  matrix products  109 us (15%)
  blocking collectives  56.7 us (8%)
  starting transfers between devices  42.1 us (6%)
  other arithmetic  33.7 us (5%)
  between operations  14.9 us (2%)
    psum x1, waiting for transfers between devices, body(): lax.psum((grad_qkv, grad_self_out, grad_cross_q, grad_cross_kv, grad_cros...  235 us
    psum x1, blocking collectives, body(): lax.psum((grad_qkv, grad_self_out, grad_cross_q, grad_cross_kv, grad_cros...  40.1 us
    all_to_all x1, waiting for transfers between devices, body(): lax.all_to_all(mixed_proj, 'seq', split_axis=3, concat_axis=1, tiled=True)  37.1 us
    unnamed x116, local copies, waits for them, and re-layouts  19.7 us
    dot_general x7, matrix products, left_dot(): lax.dot_general(left, right, (((0,), (0,)), ((), ())), preferred_element_...  19 us
    dot_general x8, matrix products, masked_scores(): jnp.einsum('qhd,khd->hqk', queries, key_heads, preferred_element_type=jnp...  16.9 us
    all_to_all x1, blocking collectives, body(): lax.all_to_all(jnp.stack(jnp.split(d_cross_q.reshape(row_count, seq_len,...  16.6 us
    all_to_all x1, waiting for transfers between devices, body(): lax.all_to_all(d_mixed, 'seq', split_axis=1, concat_axis=3, tiled=True)  16.2 us
  transfers between devices with their start and end apart: 10, of which 9 were waited for; matrix products, arithmetic and copies ran while one was open for 13% of the time, Pallas kernels for 0%

profile of v1, /device:TPU:0, one launch (start us, length us, event | category | flops | bytes accessed | tf_op | source)
XLA Modules:
  0.0 719.2 jit_solution(12766187297644499975)
XLA Ops:
  7.2 3.8 convolution_convert_fusion
  11.0 3.9 reshape.400
  15.0 2.9 copy.207
  17.9 6.3 all-to-all-start
  24.2 37.1 %all-to-all-done = bf16[2,256,3,4,128]{4,1,2,0,3:T(8,128)(2,1)} async-done(((bf16[2,256,3,4,128]{4,1,2,0,3:T(8,128)(2,1)}), bf16[2,256,3,4,128]{4,1,2,0,3:T(8,128)(2,1)}, u32[]{:S(2)}, u32[]{:S(2)}) %all-to-all-start) | async-done | bytes 1572896 | tf_op jit(solution)/shard_map/all_to_all | solution.py:128
  61.3 3.8 copy.208
  65.0 3.8 reshape.401
  68.8 2.5 slice_bitcast_fusion.2
  72.2 18.4 %while.52 = (s32[]{:T(128)}, bf16[2,1024,2,64]{1,3,2,0:T(8,128)(2,1)}, f32[2,2,1024,1]{2,1,3,0:T(2,128)S(1)}, bf16[2,1024,2,64]{1,3,2,0:T(8,128)(2,1)}, s32[2,10...) while((s32[]{:T(128)}, ...), condition=%wide.region_3.4_spmd, body=%wide.region_0.3_spmd.sunk | while | flops 565311488 | bytes 36780216 | solution.py:151
  72.9 2.9 fusion.226
  77.8 2.8 fusion.228
  82.0 2.9 fusion.226
  87.0 2.8 fusion.228
  92.6 4.1 all-to-all-start.1
  96.8 3.1 convolution_convert_fusion.1
  103.4 7.4 %all-to-all-done.1 = bf16[2,1024,1,128]{3,0,2,1:T(2,128)(2,1)} async-done(((bf16[2,1024,1,128]{3,0,2,1:T(2,128)(2,1)}), bf16[2,1024,1,128]{3,0,2,1:T(2,128)(2,1)}, u32[]{:S(2)}, u32[]{:S(2)}) %all-to-all-start.1) | async-done | bytes 524320 | tf_op jit(solution)/shard_map/all_to_all | solution.py:152
  110.8 4.2 all-to-all-start.2
  125.6 14.7 %all-to-all-done.2 = bf16[2,256,2,4,128]{4,2,1,0,3:T(2,128)(2,1)} async-done(((bf16[2,256,2,4,128]{4,2,1,0,3:T(2,128)(2,1)}), bf16[2,256,2,4,128]{4,2,1,0,3:T(2,128)(2,1)}, u32[]{:S(2)}, u32[]{:S(2)}) %all-to-all-start.2) | async-done | bytes 1048608 | tf_op jit(solution)/shard_map/all_to_all | solution.py:136
  140.3 4.4 all-to-all-start.3
  144.8 3.8 copy.213
  148.6 2.6 reshape.406
  153.4 5.4 all-to-all-done.3
  164.0 18.5 %while.53 = (s32[]{:T(128)}, bf16[2,1024,2,64]{1,3,2,0:T(8,128)(2,1)}, f32[2,2,1024,1]{2,1,3,0:T(2,128)S(1)}, bf16[2,1024,2,64]{1,3,2,0:T(8,128)(2,1)}, s32[2,10...) while((s32[]{:T(128)}, ...), condition=%wide.region_9.10_spmd, body=%wide.region_6.9_spmd.sunk | while | flops 563214336 | bytes 36792512 | solution.py:180
  164.7 2.9 fusion.230
  169.7 2.8 fusion.232
  173.9 2.9 fusion.230
  178.9 2.8 fusion.232
  184.5 4.8 all-to-all-start.4
  191.3 12.1 %all-to-all-done.4 = bf16[2,1024,1,128]{3,0,2,1:T(2,128)(2,1)} async-done(((bf16[2,1024,1,128]{3,0,2,1:T(2,128)(2,1)}), bf16[2,1024,1,128]{3,0,2,1:T(2,128)(2,1)}, u32[]{:S(2)}, u32[]{:S(2)}) %all-to-all-start.4) | async-done | bytes 524320 | tf_op jit(solution)/shard_map/all_to_all | solution.py:183
  223.1 4.3 all-to-all-start.5
  227.4 14.0 %all-to-all-done.5 = bf16[2,256,4,128]{3,1,0,2:T(8,128)(2,1)} async-done(((bf16[2,256,4,128]{3,1,0,2:T(8,128)(2,1)}), bf16[2,256,4,128]{3,1,0,2:T(8,128)(2,1)}, u32[]{:S(2)}, u32[]{:S(2)}) %all-to-all-start.5) | async-done | bytes 524320 | tf_op jit(solution)/shard_map/all_to_all | solution.py:218
  248.4 27.1 %while.54 = (s32[]{:T(128)}, bf16[2,1024,2,64]{1,3,2,0:T(8,128)(2,1)}, bf16[2,1024,2,64]{1,3,2,0:T(8,128)(2,1)}, bf16[2,1024,2,64]{1,3,2,0:T(8,128)(2,1)}, bf16[...) while((s32[]{:T(128)}, ...), condition=%wide.region_20.21_spmd, body=%wide.region_18.20_spmd.sunk | while | flops 1375336448 | bytes 86594928 | solution.py:234
  250.5 3.0 multiply_reduce_fusion.13
  253.5 2.7 multiply_convert_fusion.8
  258.6 2.5 fusion.244
  264.0 3.0 multiply_reduce_fusion.13
  267.0 2.7 multiply_convert_fusion.8
  272.2 2.5 fusion.244
  277.4 16.6 %all_to_all.140 = bf16[4,2,256,1,1,128]{5,2,1,4,3,0:T(8,128)(2,1)S(1)} all-to-all(bf16[4,2,256,1,1,128]{5,2,1,4,3,0:T(8,128)(2,1)S(1)} %pad_maximum_fusion.2), channel_id=1, replica_groups=mesh['dp'=8,'seq'=4] {'seq'}, dimensions={0} | all-to-all | bytes 1048576 | tf_op jit(solution)/shard_map/all_to_all | solution.py:243
  298.4 4.1 all-to-all-start.7
  305.9 10.2 %all-to-all-done.7 = bf16[2,256,4,128]{3,1,0,2:T(8,128)(2,1)} async-done(((bf16[2,256,4,128]{3,1,0,2:T(8,128)(2,1)}), bf16[2,256,4,128]{3,1,0,2:T(8,128)(2,1)}, u32[]{:S(2)}, u32[]{:S(2)}) %all-to-all-start.7) | async-done | bytes 524320 | tf_op jit(solution)/shard_map/all_to_all | solution.py:273
  316.1 4.3 all-to-all-start.9
  325.5 27.0 %while.55 = (s32[]{:T(128)}, bf16[2,1024,2,64]{1,3,2,0:T(8,128)(2,1)}, bf16[2,1024,2,64]{1,3,2,0:T(8,128)(2,1)}, bf16[2,1024,2,64]{1,3,2,0:T(8,128)(2,1)}, bf16[...) while((s32[]{:T(128)}, ...), condition=%wide.region_25.26_spmd, body=%wide.region_23.25_spmd.sunk | while | flops 1377433600 | bytes 86582632 | solution.py:289
  327.5 3.0 multiply_reduce_fusion.14
  330.5 2.7 multiply_convert_fusion.9
  335.7 2.5 fusion.257
  341.0 3.0 multiply_reduce_fusion.14
  344.0 2.7 multiply_convert_fusion.9
  349.2 2.5 fusion.257
  352.6 2.8 pad_maximum_fusion
  355.3 5.1 copy.228
  360.4 5.1 all-to-all-start.8
  365.9 2.5 fusion.134
  368.4 5.2 fusion.153
  373.6 3.5 fusion.150
  385.3 16.2 %all-to-all-done.8 = bf16[2,1024,3,1,128]{4,0,3,2,1:T(2,128)(2,1)} async-done(((bf16[2,1024,3,1,128]{4,0,3,2,1:T(2,128)(2,1)}), bf16[2,1024,3,1,128]{4,0,3,2,1:T(2,128)(2,1)}, u32[]{:S(2)}, u32[]{:S(2)}) %all-to-all-start.8) | async-done | bytes 1572896 | tf_op jit(solution)/shard_map/all_to_all | solution.py:295
  405.4 2.8 reshape.418
  408.3 2.7 convolution_bitcast_fusion
  411.7 40.1 %all-reduce = (f32[512]{0:T(512)}, f32[512]{0:T(512)}, f32[512]{0:T(512)}, f32[512]{0:T(512)}, f32[512]{0:T(512)}, /*index=5*/f32[512]{0:T(512)}) all-reduce(f32[512]{0:T(512)S(1)} %get-tuple-element.334, f32[512]{0:T(512)S(1)} %get-tuple-element.341, f32[512]{0:T(512)S(1)} %copy-done.71, ...), channel_id=1, replica_groups=mesh['dp'=8,'seq'=4] {'dp','seq'}, use_global_device_ids=true, to_apply=%region_34.35 | all-reduce | flops 3072 | bytes 24576 | tf_op jit(solution)/shard_map/psum | solution.py:302
  453.4 3.3 fusion.120
  456.7 3.8 convolution_add_fusion.3
  460.5 234.7 %all-reduce.4.cloned.1.call-done = (f32[512,1536]{0,1:T(8,128)}, f32[512,512]{1,0:T(8,128)}, f32[512,512]{1,0:T(8,128)}, f32[512,1024]{0,1:T(8,128)}, f32[512,51...) async-done(((f32[512,1536]{0,1:T(8,128)}, f32[512,512]{1,0:T(8,128)}, f32[512,512]{1,0:T(8,128)}, f32[512,1024]{0,1:T(8,128)}, f32[512,512]{1,0:T(8,128)}, ...) | async-done | bytes 16777232 | tf_op jit(solution)/shard_map/psum | solution.py:302
  695.3 3.7 copy.235
  700.8 2.4 copy.340
  (323 shorter events, 129.3 us)
Async XLA Ops:
  7.2 200.5 %copy-start = (bf16[512,2048]{1,0:T(8,128)(2,1)S(1)}, bf16[512,2048]{1,0:T(8,128)(2,1)}, u32[]{:S(2)}) copy-start(bf16[512,2048]{1,0:T(8,128)(2,1)} %param.36) | copy-start | bytes 6291460
  17.9 43.4 %all-to-all-start = ((bf16[2,256,3,4,128]{4,1,2,0,3:T(8,128)(2,1)}), bf16[2,256,3,4,128]{4,1,2,0,3:T(8,128)(2,1)}, u32[]{:S(2)}, u32[]{:S(2)}) async-start(bf16[2,256,3,4,128]{4,1,2,0,3:T(8,128)(2,1)} %copy.207), calls=%async_computation | async-start | bytes 3145728 | tf_op jit(solution)/shard_map/all_to_all | solution.py:128
  65.0 7.2 %copy-start.53 = (s32[2,1024]{1,0:T(2,128)S(1)}, s32[2,1024]{1,0:T(2,128)}, u32[]{:S(2)}) copy-start(s32[2,1024]{1,0:T(2,128)} %param.28) | copy-start | bytes 24580
  90.6 12.8 %copy-start.56 = (f32[2,2,1024,1]{2,1,3,0:T(2,128)}, f32[2,2,1024,1]{2,1,3,0:T(2,128)S(1)}, u32[]{:S(2)}) copy-start(f32[2,2,1024,1]{2,1,3,0:T(2,128)S(1)} %get-tuple-element.800) | copy-start | bytes 49156
  92.6 18.2 %all-to-all-start.1 = ((bf16[2,1024,1,128]{3,0,2,1:T(2,128)(2,1)}), bf16[2,1024,1,128]{3,0,2,1:T(2,128)(2,1)}, u32[]{:S(2)}, u32[]{:S(2)}) async-start(bf16[2,1024,1,128]{3,0,2,1:T(2,128)(2,1)} %copy.209), calls=%async_computation.1 | async-start | bytes 1048576 | tf_op jit(solution)/shard_map/all_to_all | solution.py:152
  103.4 16.0 %copy-start.67 = (f32[512]{0:T(512)S(1)}, f32[512]{0:T(512)}, u32[]{:S(2)}) copy-start(f32[512]{0:T(512)} %param.38) | copy-start | bytes 6148
  103.4 16.0 %copy-start.73 = (f32[512]{0:T(512)S(1)}, f32[512]{0:T(512)}, u32[]{:S(2)}) copy-start(f32[512]{0:T(512)} %param.39) | copy-start | bytes 6148
  110.8 29.5 %all-to-all-start.2 = ((bf16[2,256,2,4,128]{4,2,1,0,3:T(2,128)(2,1)}), bf16[2,256,2,4,128]{4,2,1,0,3:T(2,128)(2,1)}, u32[]{:S(2)}, u32[]{:S(2)}) async-start(bf16[2,256,2,4,128]{4,2,1,0,3:T(2,128)(2,1)} %copy.212), calls=%async_computation.2 | async-start | bytes 2097152 | tf_op jit(solution)/shard_map/all_to_all | solution.py:136
  140.3 18.5 %all-to-all-start.3 = ((bf16[2,256,1,4,128]{4,1,0,2,3:T(8,128)(2,1)}), bf16[2,256,1,4,128]{4,1,0,2,3:T(8,128)(2,1)}, u32[]{:S(2)}, u32[]{:S(2)}) async-start(bf16[2,256,1,4,128]{4,1,0,2,3:T(8,128)(2,1)} %copy.214), calls=%async_computation.3 | async-start | bytes 1048576 | tf_op jit(solution)/shard_map/all_to_all | solution.py:170
  144.8 19.2 %copy-start.55 = (s32[2,1024]{1,0:T(2,128)S(1)}, s32[2,1024]{1,0:T(2,128)}, u32[]{:S(2)}) copy-start(s32[2,1024]{1,0:T(2,128)} %param.29) | copy-start | bytes 24580
  164.0 25.4 %copy-start.66 = (f32[512]{0:T(512)S(1)}, f32[512]{0:T(512)}, u32[]{:S(2)}) copy-start(f32[512]{0:T(512)} %param.42) | copy-start | bytes 6148
  184.5 23.2 %copy-start.62 = (f32[512]{0:T(512)S(1)}, f32[512]{0:T(512)}, u32[]{:S(2)}) copy-start(f32[512]{0:T(512)} %param.40) | copy-start | bytes 6148
  184.5 23.2 %copy-start.64 = (f32[512]{0:T(512)S(1)}, f32[512]{0:T(512)}, u32[]{:S(2)}) copy-start(f32[512]{0:T(512)} %param.41) | copy-start | bytes 6148
  184.5 18.9 %all-to-all-start.4 = ((bf16[2,1024,1,128]{3,0,2,1:T(2,128)(2,1)}), bf16[2,1024,1,128]{3,0,2,1:T(2,128)(2,1)}, u32[]{:S(2)}, u32[]{:S(2)}) async-start(bf16[2,1024,1,128]{3,0,2,1:T(2,128)(2,1)} %copy.216), calls=%async_computation.4 | async-start | bytes 1048576 | tf_op jit(solution)/shard_map/all_to_all | solution.py:183
  207.4 10.1 %copy-start.2 = (f32[512,512]{1,0:T(8,128)}, f32[512,512]{1,0:T(8,128)S(1)}, u32[]{:S(2)}) copy-start(f32[512,512]{1,0:T(8,128)S(1)} %get-tuple-element.455) | copy-start | bytes 3145732
  207.4 10.1 %copy-start.58 = (f32[512]{0:T(512)}, f32[512]{0:T(512)S(1)}, u32[]{:S(2)}) copy-start(f32[512]{0:T(512)S(1)} %broadcast_multiply_fusion.6) | copy-start | bytes 6148
  207.7 9.8 %copy-start.60 = (f32[512]{0:T(512)}, f32[512]{0:T(512)S(1)}, u32[]{:S(2)}) copy-start(f32[512]{0:T(512)S(1)} %add_rsqrt_fusion.1) | copy-start | bytes 6148
  209.4 4.0 copy-start.23
  209.4 2.8 copy-start.70
  217.9 29.6 %copy-start.8 = (f32[512,512]{1,0:T(8,128)}, f32[512,512]{1,0:T(8,128)S(1)}, u32[]{:S(2)}) copy-start(f32[512,512]{1,0:T(8,128)S(1)} %subtract_multiply_fusion.1) | copy-start | bytes 3145732
  217.9 30.5 %copy-start.4 = (bf16[2,1024,2,64]{1,3,2,0:T(8,128)(2,1)S(1)}, bf16[2,1024,2,64]{1,3,2,0:T(8,128)(2,1)}, u32[]{:S(2)}) copy-start(bf16[2,1024,2,64]{1,3,2,0:T(8,128)(2,1)} %get-tuple-element.858) | copy-start | bytes 1572868
  217.9 30.5 %copy-start.7 = (bf16[2,1024,2,64]{1,3,2,0:T(8,128)(2,1)S(1)}, bf16[2,1024,2,64]{1,3,2,0:T(8,128)(2,1)}, u32[]{:S(2)}) copy-start(bf16[2,1024,2,64]{1,3,2,0:T(8,128)(2,1)} %get-tuple-element.861) | copy-start | bytes 1572868
  223.1 18.4 %all-to-all-start.5 = ((bf16[2,256,4,128]{3,1,0,2:T(8,128)(2,1)}), bf16[2,256,4,128]{3,1,0,2:T(8,128)(2,1)}, u32[]{:S(2)}, u32[]{:S(2)}) async-start(bf16[2,256,4,128]{3,1,0,2:T(8,128)(2,1)} %copy.219), calls=%async_computation.5 | async-start | bytes 1048576 | tf_op jit(solution)/shard_map/all_to_all | solution.py:218
  253.5 2.7 copy-start.30
  257.1 4.1 copy-start.31
  258.6 2.6 copy-start.43
  267.0 2.7 copy-start.30
  270.6 4.1 copy-start.31
  272.2 2.6 copy-start.43
  275.6 18.8 %copy-start.9 = (f32[512,512]{1,0:T(8,128)S(1)}, f32[512,512]{1,0:T(8,128)}, u32[]{:S(2)}) copy-start(f32[512,512]{1,0:T(8,128)} %copy-done.8) | copy-start | bytes 3145732
  294.0 2.9 copy-start.48
  296.9 5.7 copy-start.11
  298.4 17.8 %all-to-all-start.7 = ((bf16[2,256,4,128]{3,1,0,2:T(8,128)(2,1)}), bf16[2,256,4,128]{3,1,0,2:T(8,128)(2,1)}, u32[]{:S(2)}, u32[]{:S(2)}) async-start(bf16[2,256,4,128]{3,1,0,2:T(8,128)(2,1)} %copy.226), calls=%async_computation.7 | async-start | bytes 1048576 | tf_op jit(solution)/shard_map/all_to_all | solution.py:273
  303.8 21.7 %copy-start.5 = (bf16[2,1024,2,64]{1,3,2,0:T(8,128)(2,1)S(1)}, bf16[2,1024,2,64]{1,3,2,0:T(8,128)(2,1)}, u32[]{:S(2)}) copy-start(bf16[2,1024,2,64]{1,3,2,0:T(8,128)(2,1)} %get-tuple-element.859) | copy-start | bytes 1572868
  303.8 21.7 %copy-start.6 = (bf16[2,1024,2,64]{1,3,2,0:T(8,128)(2,1)S(1)}, bf16[2,1024,2,64]{1,3,2,0:T(8,128)(2,1)}, u32[]{:S(2)}) copy-start(bf16[2,1024,2,64]{1,3,2,0:T(8,128)(2,1)} %get-tuple-element.860) | copy-start | bytes 1572868
  303.9 21.7 %copy-start.57 = (f32[2,2,1024,1]{2,1,3,0:T(2,128)S(1)}, f32[2,2,1024,1]{2,1,3,0:T(2,128)}, u32[]{:S(2)}) copy-start(f32[2,2,1024,1]{2,1,3,0:T(2,128)} %copy-done.56) | copy-start | bytes 49156
  316.1 44.3 %all-to-all-start.9 = ((bf16[2,1024,2,1,128]{4,0,3,2,1:T(2,128)(2,1)}), bf16[2,1024,2,1,128]{4,0,3,2,1:T(2,128)(2,1)}, u32[]{:S(2)}, u32[]{:S(2)}) async-start(bf16[2,1024,2,1,128]{4,0,3,2,1:T(2,128)(2,1)} %copy.231), calls=%async_computation.9 | async-start | bytes 2097152 | tf_op jit(solution)/shard_map/all_to_all | solution.py:257
  330.5 2.7 copy-start.36
  334.1 4.1 copy-start.37
  335.7 2.6 copy-start.39
  344.0 2.7 copy-start.36
  347.6 4.1 copy-start.37
  349.2 2.6 copy-start.39
  352.5 13.3 %copy-start.10 = (f32[512,512]{1,0:T(8,128)S(1)}, f32[512,512]{1,0:T(8,128)}, u32[]{:S(2)}) copy-start(f32[512,512]{1,0:T(8,128)} %copy-done.8) | copy-start | bytes 3145732
  355.3 13.1 %copy-start.3 = (f32[512,512]{1,0:T(8,128)S(1)}, f32[512,512]{1,0:T(8,128)}, u32[]{:S(2)}) copy-start(f32[512,512]{1,0:T(8,128)} %copy-done.2) | copy-start | bytes 3145732
  355.3 13.1 %copy-start.59 = (f32[512]{0:T(512)S(1)}, f32[512]{0:T(512)}, u32[]{:S(2)}) copy-start(f32[512]{0:T(512)} %copy-done.58) | copy-start | bytes 6148
  355.3 13.1 %copy-start.61 = (f32[512]{0:T(512)S(1)}, f32[512]{0:T(512)}, u32[]{:S(2)}) copy-start(f32[512]{0:T(512)} %copy-done.60) | copy-start | bytes 6148
  355.3 13.1 %copy-start.63 = (f32[512]{0:T(512)S(1)}, f32[512]{0:T(512)}, u32[]{:S(2)}) copy-start(f32[512]{0:T(512)} %param.40) | copy-start | bytes 6148
  355.3 13.1 %copy-start.65 = (f32[512]{0:T(512)S(1)}, f32[512]{0:T(512)}, u32[]{:S(2)}) copy-start(f32[512]{0:T(512)} %param.41) | copy-start | bytes 6148
  360.4 41.0 %all-to-all-start.8 = ((bf16[2,1024,3,1,128]{4,0,3,2,1:T(2,128)(2,1)}), bf16[2,1024,3,1,128]{4,0,3,2,1:T(2,128)(2,1)}, u32[]{:S(2)}, u32[]{:S(2)}) async-start(bf16[2,1024,3,1,128]{4,0,3,2,1:T(2,128)(2,1)} %copy.228), calls=%async_computation.8 | async-start | bytes 3145728 | tf_op jit(solution)/shard_map/all_to_all | solution.py:295
  365.5 329.8 %all-reduce.4.cloned.1.call-start = ((), (), s32[]{:S(2)}) async-start(), calls=%async_computation.10 | async-start | bytes 33554432 | tf_op jit(solution)/shard_map/psum | solution.py:302
  368.4 5.2 copy-start.24
  368.4 5.2 copy-start.51
  373.6 3.5 copy-start.12
  373.6 3.5 copy-start.20
  373.6 4.9 copy-start.28
  373.6 4.9 copy-start.74
  378.5 4.6 copy-start.54
  385.3 23.0 %copy-start.49 = (bf16[2,256,512]{2,1,0:T(8,128)(2,1)S(1)}, bf16[2,256,512]{2,1,0:T(8,128)(2,1)}, u32[]{:S(2)}) copy-start(bf16[2,256,512]{2,1,0:T(8,128)(2,1)} %param.26) | copy-start | bytes 1572868
  695.2 3.7 copy-start.29
  698.9 6.5 copy-start.52
  700.8 5.7 copy-start.26
  706.4 3.7 copy-start.25
  706.4 5.7 copy-start.1
  (44 other events, 69.6 us)
Sparse Core Ops, SparseCore 0:
  411.2 284.0 all-reduce.3
